TPU v7x, 256 devices: a whole 4x4x8 slice. The times are simulated.
256 devices in a mesh: wide: 16 (over z, core), grow: 4 (over y), gcol: 4 (over x).
Axes of the slice: x: 4, y: 4, z: 8, core: 2. Of those that a mesh axis runs over, the one named last changes fastest.
Arguments:
- diag_block: float32 [16, 1024, 1024], P('wide', ('grow', 'gcol')), as said below
- lower_block: float32 [16, 3072, 1024], P('wide', ('grow', 'gcol')), may hold values from -0.1875 to 0.1875
- trailing_block: float32 [16, 3072, 3072], P('wide', 'grow', 'gcol'), as said below
- parent_front: float32 [4, 2048, 8192], P('grow', 'wide', 'gcol'), may hold values from -3 to 3
- row_map: int32 [16, 24], replicated, may hold values from 0 to 63, as said below
Outputs:
- factor: float32 [16, 1024, 1024], P('wide', ('grow', 'gcol'))
- panel: float32 [16, 3072, 1024], P('wide', ('grow', 'gcol'))
- parent: float32 [4, 2048, 8192], P('grow', 'wide', 'gcol')
Inputs may be any that keep to these rules, and one draw needn't show every extreme that they name: Each diag_block[g] is symmetric and positive definite. Each trailing_block[g] is symmetric. `row_map`: the blocks of one child are distinct, and child block b goes to a grandparent block p with p // 16 equal to b // 6.
All inputs are finite; a program needn't handle non-finite values.
Results may differ from a plain program's by a relative error of at most 0.0003.
Values sent between devices are 32-bit elements; how exact they have to be, the bound alone decides.
No kernel may reach another device: no remote copies, remote signals or barrier semaphores. Data moves between devices by JAX's collectives and lax.ppermute only.
A program may use at most 128 MiB of HBM per device.

v0:
```python
import jax
import jax.numpy as jnp
from jax import lax
from jax.sharding import PartitionSpec as P

BLOCK = 128


def cut_rows(length, count):
    unit = 8 if length >= 8 * count else 1
    return [length // unit * k // count * unit for k in range(1, count)]


def gather_in_order(x, axes, turns):
    tiles = x
    for k in turns:
        tiles = lax.all_gather(tiles, axes[k])
    done = turns[::-1]
    back = [done.index(k) for k in range(len(axes))]
    tiles = tiles.transpose(*back, *range(len(axes), tiles.ndim))
    return tiles.reshape(-1, *x.shape)


def laid_out(tiles, dim):
    dims = list(tiles.shape[1:])
    dims[dim] *= tiles.shape[0]
    return jnp.moveaxis(tiles, 0, dim).reshape(dims)


def gather_at_once(x, axes, dim):
    cut = max(range(max(1, x.ndim - 1)), key=lambda d: x.shape[d])
    count, gathered = (len(axes), [])
    for initial, section in enumerate(jnp.split(x, cut_rows(x.shape[cut], count), axis=cut)):
        if section.size:
            turns = [(initial - k) % count for k in range(count)]
            gathered.append(gather_in_order(section, axes, turns))
    return laid_out(jnp.concatenate(gathered, axis=cut + 1), dim)


def filled_up(lines, peers):
    spare = -lines.shape[0] % peers
    if not spare:
        return lines
    return jnp.concatenate([lines, jnp.zeros((spare, *lines.shape[1:]), lines.dtype)])


def broadcast_by_parts(x, axis, root):
    lines = jnp.where(lax.axis_index(axis) == root, x, jnp.zeros_like(x)).reshape(
        -1, *x.shape[1:][-1:]
    )
    padded = filled_up(lines, lax.axis_size(axis))
    own = lax.psum_scatter(padded, axis, scatter_dimension=0, tiled=True)
    return lax.all_gather(own, axis, axis=0, tiled=True)[: len(lines)].reshape(x.shape)


def local(diag_block, lower_block, trailing_block, parent_front, row_map):
    highest = lax.Precision.HIGHEST
    whole = gather_at_once(diag_block[0], ("grow", "gcol"), 0)
    factor = jnp.linalg.cholesky(whole)
    share = diag_block.shape[1]
    factor_rows = lax.dynamic_slice_in_dim(
        factor, lax.axis_index(("grow", "gcol")) * share, share, 0
    )
    panel = jax.scipy.linalg.solve_triangular(factor, lower_block[0].T, lower=True).T
    row_part = lax.all_gather(panel, "gcol", axis=0, tiled=True)
    column_index = lax.axis_index("gcol")
    col_part = broadcast_by_parts(row_part, "grow", column_index)
    update = lax.dot_general(
        row_part,
        col_part,
        (((1,), (1,)), ((), ())),
        precision=highest,
        preferred_element_type=jnp.float32,
    )
    schur = trailing_block[0] - update
    owners = lax.axis_size("wide")
    child = lax.axis_index("wide")
    row_index = lax.axis_index("grow")
    width_blocks = schur.shape[0] // BLOCK
    quarter_blocks = parent_front.shape[1] * owners // BLOCK
    column_blocks = parent_front.shape[2] // BLOCK
    row_local = (
        lax.dynamic_slice_in_dim(row_map, row_index * width_blocks, width_blocks, 1)
        % quarter_blocks
    )
    col_local = (
        lax.dynamic_slice_in_dim(row_map, column_index * width_blocks, width_blocks, 1)
        % column_blocks
    )
    grid = jnp.arange(column_blocks, dtype=jnp.int32)
    mine_rows = lax.dynamic_slice_in_dim(row_local, child, 1, 0)[0]
    mine_cols = lax.dynamic_slice_in_dim(col_local, child, 1, 0)[0]
    col_place = (mine_cols[None, :] == grid[:, None]).astype(jnp.float32)
    pieces = schur.reshape(width_blocks, BLOCK, width_blocks, BLOCK)
    count = parent_front.shape[1] * lax.axis_size("wide")
    blocks = count // BLOCK
    wanted = jnp.arange(blocks, dtype=jnp.int32)
    row_place = (mine_rows[None, :] == wanted[:, None]).astype(jnp.float32)
    placed = jnp.einsum("pb,bxcy->pxcy", row_place, pieces, precision=highest)
    spread = jnp.einsum("pxcy,qc->pxqy", placed, col_place, precision=highest)
    summed = lax.psum_scatter(
        spread.reshape(count, column_blocks * BLOCK), "wide", scatter_dimension=0, tiled=True
    )
    parent = parent_front + summed[None]
    return (factor_rows[None], panel[None], parent)


def solution(mesh):
    placed = (
        P("wide", ("grow", "gcol"), None),
        P("wide", ("grow", "gcol"), None),
        P("wide", "grow", "gcol"),
        P("grow", "wide", "gcol"),
        P(),
    )
    return jax.shard_map(
        local,
        mesh=mesh,
        in_specs=placed,
        out_specs=(
            P("wide", ("grow", "gcol"), None),
            P("wide", ("grow", "gcol"), None),
            P("grow", "wide", "gcol"),
        ),
        check_vma=False,
    )
```

profile of v0, /device:TPU:2, one launch (start us, length us, event | category | flops | bytes accessed | tf_op | source)
XLA Modules:
  0.0 715.4 jit_solution(11808410995972547139)
XLA Ops:
  8.2 14.0 %all_gather.26 = f32[4,32,1024]{2,1,0:T(8,128)} all-gather(f32[1,32,1024]{2,1,0:T(8,128)S(1)} %get-tuple-element.27), channel_id=1, replica_groups=mesh['wide'=16,'grow'=4,'gcol'=4] {'grow'}, dimensions={0}, use_global_device_ids=true | all-gather | bytes 655360 | tf_op jit(solution)/shard_map/all_gather | solution.py:17
  22.3 13.6 %all_gather.29 = f32[4,32,1024]{2,1,0:T(8,128)} all-gather(f32[1,32,1024]{2,1,0:T(8,128)S(1)} %get-tuple-element.28), channel_id=1, replica_groups=mesh['wide'=16,'grow'=4,'gcol'=4] {'gcol'}, dimensions={0}, use_global_device_ids=true | all-gather | bytes 655360 | tf_op jit(solution)/shard_map/all_gather | solution.py:17
  36.0 21.8 %all-gather.11.cloned.1.call-done = f32[16,32,1024]{2,1,0:T(8,128)} async-done(((f32[4,32,1024]{2,1,0:T(8,128)}), f32[16,32,1024]{2,1,0:T(8,128)}) %all-gather.11.cloned.1.call-update) | async-done | bytes 2097168 | tf_op jit(solution)/shard_map/all_gather | solution.py:17
  57.8 1.7 copy.13
  59.5 34.5 %all-gather.13.cloned.1.call-done = f32[16,32,1024]{2,1,0:T(8,128)} async-done(((f32[4,32,1024]{2,1,0:T(8,128)}), f32[16,32,1024]{2,1,0:T(8,128)}) %all-gather.13.cloned.1.call-update) | async-done | bytes 2097168 | tf_op jit(solution)/shard_map/all_gather | solution.py:17
  94.0 4.1 pad_maximum_fusion
  98.1 5.3 copy.14
  103.4 4.4 fusion.2
  107.9 1.9 copy-done.1
  109.8 11.7 %cholesky.223 = f32[128,128]{1,0:T(8,128)S(1)} custom-call(f32[128,128]{1,0:T(8,128)S(1)} %cholesky.580), custom_call_target="Cholesky" | custom-call | tf_op jit(solution)/shard_map/jit(cholesky)/cholesky | solution.py:59
  121.5 9.8 %custom-call.63 = f32[1,128,128]{1,2,0:T(8,128)S(1)} custom-call(f32[1,128,128]{2,1,0:T(8,128)S(1)} %get-tuple-element.75), custom_call_target="InvertDiagBlocksLowerTriangular" | custom-call | tf_op jit(solution)/shard_map/jit(cholesky)/cholesky | solution.py:59
  131.4 2.5 cholesky.255
  133.9 2.4 constant_dynamic-update-slice_fusion.25
  136.2 1.5 convolution_subtract_fusion
  137.8 11.9 %cholesky.244 = f32[128,128]{1,0:T(8,128)S(1)} custom-call(f32[128,128]{1,0:T(8,128)S(1)} %cholesky.584), custom_call_target="Cholesky" | custom-call | tf_op jit(solution)/shard_map/jit(cholesky)/cholesky | solution.py:59
  150.3 9.8 %custom-call.64 = f32[1,128,128]{1,2,0:T(8,128)S(1)} custom-call(f32[1,128,128]{2,1,0:T(8,128)S(1)} %get-tuple-element.72), custom_call_target="InvertDiagBlocksLowerTriangular" | custom-call | tf_op jit(solution)/shard_map/jit(cholesky)/cholesky | solution.py:59
  160.1 1.2 convolution_dynamic-update-slice_fusion
  161.4 2.1 convolution_subtract_fusion.1
  163.5 11.7 %cholesky.468 = f32[128,128]{1,0:T(8,128)S(1)} custom-call(f32[128,128]{1,0:T(8,128)S(1)} %cholesky.589), custom_call_target="Cholesky" | custom-call | tf_op jit(solution)/shard_map/jit(cholesky)/cholesky | solution.py:59
  176.5 9.8 %custom-call.65 = f32[1,128,128]{1,2,0:T(8,128)S(1)} custom-call(f32[1,128,128]{2,1,0:T(8,128)S(1)} %get-tuple-element.69), custom_call_target="InvertDiagBlocksLowerTriangular" | custom-call | tf_op jit(solution)/shard_map/jit(cholesky)/cholesky | solution.py:59
  186.3 1.2 convolution_dynamic-update-slice_fusion.1
  187.4 2.3 convolution_subtract_fusion.2
  189.8 11.9 %cholesky.487 = f32[128,128]{1,0:T(8,128)S(1)} custom-call(f32[128,128]{1,0:T(8,128)S(1)} %cholesky.594), custom_call_target="Cholesky" | custom-call | tf_op jit(solution)/shard_map/jit(cholesky)/cholesky | solution.py:59
  203.0 9.8 %custom-call.66 = f32[1,128,128]{1,2,0:T(8,128)S(1)} custom-call(f32[1,128,128]{2,1,0:T(8,128)S(1)} %get-tuple-element.66), custom_call_target="InvertDiagBlocksLowerTriangular" | custom-call | tf_op jit(solution)/shard_map/jit(cholesky)/cholesky | solution.py:59
  213.9 2.3 convolution_subtract_fusion.3
  216.2 11.7 %cholesky.506 = f32[128,128]{1,0:T(8,128)S(1)} custom-call(f32[128,128]{1,0:T(8,128)S(1)} %cholesky.599), custom_call_target="Cholesky" | custom-call | tf_op jit(solution)/shard_map/jit(cholesky)/cholesky | solution.py:59
  229.2 10.2 %custom-call.67 = f32[1,128,128]{1,2,0:T(8,128)S(1)} custom-call(f32[1,128,128]{2,1,0:T(8,128)S(1)} %get-tuple-element.63), custom_call_target="InvertDiagBlocksLowerTriangular" | custom-call | tf_op jit(solution)/shard_map/jit(cholesky)/cholesky | solution.py:59
  240.5 2.3 convolution_subtract_fusion.4
  242.8 11.7 %cholesky.526 = f32[128,128]{1,0:T(8,128)S(1)} custom-call(f32[128,128]{1,0:T(8,128)S(1)} %cholesky.604), custom_call_target="Cholesky" | custom-call | tf_op jit(solution)/shard_map/jit(cholesky)/cholesky | solution.py:59
  255.7 9.8 %custom-call.68 = f32[1,128,128]{1,2,0:T(8,128)S(1)} custom-call(f32[1,128,128]{2,1,0:T(8,128)S(1)} %get-tuple-element.60), custom_call_target="InvertDiagBlocksLowerTriangular" | custom-call | tf_op jit(solution)/shard_map/jit(cholesky)/cholesky | solution.py:59
  266.5 2.0 convolution_subtract_fusion.5
  268.5 11.9 %cholesky.546 = f32[128,128]{1,0:T(8,128)S(1)} custom-call(f32[128,128]{1,0:T(8,128)S(1)} %cholesky.609), custom_call_target="Cholesky" | custom-call | tf_op jit(solution)/shard_map/jit(cholesky)/cholesky | solution.py:59
  281.7 9.8 %custom-call.69 = f32[1,128,128]{1,2,0:T(8,128)S(1)} custom-call(f32[1,128,128]{2,1,0:T(8,128)S(1)} %get-tuple-element.57), custom_call_target="InvertDiagBlocksLowerTriangular" | custom-call | tf_op jit(solution)/shard_map/jit(cholesky)/cholesky | solution.py:59
  292.3 1.8 convolution_subtract_fusion.13
  294.1 11.7 %cholesky.564 = f32[128,128]{1,0:T(8,128)S(1)} custom-call(f32[128,128]{1,0:T(8,128)S(1)} %convolution_subtract_fusion.13), custom_call_target="Cholesky" | custom-call | tf_op jit(solution)/shard_map/jit(cholesky)/cholesky | solution.py:59
  312.8 6.7 fusion.3
  319.5 23.2 %while.1 = (s32[]{:T(128)}, f32[1024,1024]{1,0:T(8,128)}, s32[8,2]{0,1:T(2,128)S(1)}, f32[8,128,128]{2,1,0:T(8,128)S(1)}, s32[]{:T(128)}) while((s32[]{:T(128)}, f32[1024,1024]{1,0:T(8,128)}, s32[8,2]{0,1:T(2,128)S(1)}, f32[8,128,128]{2,1,0:T(8,128)S(1)}, s32[]{:T(128)}) %tuple.67), condition=%wide.while_cond, body=%wide.while_body.sunk | while | flops 2 | bytes 131189 | solution.py:64
  320.1 2.3 bitcast_dynamic-update-slice_fusion.2
  323.0 2.3 bitcast_dynamic-update-slice_fusion.2
  325.9 2.3 bitcast_dynamic-update-slice_fusion.2
  328.8 2.3 bitcast_dynamic-update-slice_fusion.2
  331.7 2.3 bitcast_dynamic-update-slice_fusion.2
  334.6 2.3 bitcast_dynamic-update-slice_fusion.2
  337.6 2.3 bitcast_dynamic-update-slice_fusion.2
  340.5 2.2 bitcast_dynamic-update-slice_fusion.2
  342.7 78.8 %custom-call.70 = f32[8,128,128]{1,2,0:T(8,128)S(1)} custom-call(f32[8,128,128]{2,1,0:T(8,128)S(1)} %get-tuple-element.10), custom_call_target="InvertDiagBlocksLowerTriangular" | custom-call | tf_op jit(solution)/shard_map/jit(_solve_triangular)/triangular_solve | solution.py:64
  423.1 1.2 convolution_subtract_fusion.12
  424.6 1.3 convolution_subtract_fusion.11
  426.2 1.4 convolution_subtract_fusion.9
  427.9 1.6 convolution_subtract_fusion.8
  429.7 1.6 convolution_subtract_fusion.7
  431.6 1.8 convolution_subtract_fusion.6
  434.6 41.4 %all-gather.7.cloned.1.call-done = f32[768,1024]{1,0:T(8,128)} async-done(((f32[192,1024]{1,0:T(8,128)}), f32[768,1024]{1,0:T(8,128)}) %all-gather.7.cloned.1.call-update) | async-done | bytes 3145744 | tf_op jit(solution)/shard_map/all_gather | solution.py:65
  476.0 2.3 broadcast_select_fusion
  478.4 44.0 %reduce-scatter.3.cloned.1.call-done = f32[192,1024]{1,0:T(8,128)} async-done(((f32[768,1024]{1,0:T(8,128)}), f32[192,1024]{1,0:T(8,128)}) %reduce-scatter.3.cloned.1.call-update) | async-done | bytes 786448 | tf_op jit(solution)/shard_map/reduce_scatter | solution.py:52
  522.5 43.4 %all-gather.9.cloned.1.call-done = f32[768,1024]{1,0:T(8,128)} async-done(((f32[192,1024]{1,0:T(8,128)}), f32[768,1024]{1,0:T(8,128)}) %all-gather.9.cloned.1.call-update) | async-done | bytes 3145744 | tf_op jit(solution)/shard_map/all_gather | solution.py:53
  565.9 11.4 %bitcast_subtract_fusion = f32[768,768]{1,0:T(8,128)} fusion(f32[1,768,768]{2,1,0:T(8,128)} %param.7, f32[768,1024]{1,0:T(8,128)S(1)} %copy-done, f32[768,1024]{1,0:T(8,128)} %all-gather.9.cloned.1.call-done), kind=kOutput, calls=%fused_computation.13 | convolution fusion | flops 7248347136 | bytes 11010048 | tf_op jit(solution)/shard_map/dot_general | solution.py:68
  577.3 2.5 reshape.103
  579.8 4.0 fusion.4
  583.8 9.9 %fusion = f32[16,16,128,128]{3,0,2,1:T(8,128)S(1)} fusion(f32[16,128,6,128]{3,0,2,1:T(8,128)S(1)} %fusion.4, s32[6]{0:T(128)S(1)} %fusion.71), kind=kOutput, calls=%fused_computation.3 | convolution fusion | flops 301989984 | bytes 23068696 | tf_op jit(solution)/shard_map/pxcy,qc->pxqy/dot_general | solution.py:100
  593.7 11.2 %copy.25 = f32[256,8,16,128]{3,1,2,0:T(8,128)} copy(f32[256,8,16,128]{3,2,1,0:T(8,128)S(1)} %bitcast.141) | data formatting | bytes 33554432
  605.0 1.8 dynamic-slice_bitcast_fusion
  606.7 99.1 %reduce-scatter.5.cloned.1.call-done = f32[128,2048]{1,0:T(8,128)} async-done(((f32[2048,2048]{1,0:T(8,128)}), f32[128,2048]{1,0:T(8,128)}) %reduce-scatter.5.cloned.1.call-update) | async-done | bytes 1048592 | tf_op jit(solution)/shard_map/reduce_scatter | solution.py:101
  705.8 2.3 bitcast_add_fusion.1
  (81 shorter events, 23.2 us)
Async XLA Ops:
  7.2 50.6 %all-gather.11.cloned.1.call-start = ((), (), s32[]{:S(2)}) async-start(), calls=%async_computation.6 | async-start | bytes 2621440 | tf_op jit(solution)/shard_map/all_gather | solution.py:17
  22.3 71.7 %all-gather.13.cloned.1.call-start = ((), (), s32[]{:S(2)}) async-start(), calls=%async_computation.7 | async-start | bytes 2621440 | tf_op jit(solution)/shard_map/all_gather | solution.py:17
  35.9 440.1 %all-gather.7.cloned.1.call-start = ((), (), s32[]{:S(2)}) async-start(), calls=%async_computation.2 | async-start | bytes 3932160 | tf_op jit(solution)/shard_map/all_gather | solution.py:65
  107.9 1.9 copy-start.1
  312.8 108.7 %copy-start.4 = (f32[1,192,1024]{2,1,0:T(8,128)S(1)}, f32[1,192,1024]{2,1,0:T(8,128)}, u32[]{:S(2)}) copy-start(f32[1,192,1024]{2,1,0:T(8,128)} %param.6) | copy-start | bytes 2359300
  433.6 0.9 copy-start.3
  434.6 87.8 %reduce-scatter.3.cloned.1.call-start = ((), (), s32[]{:S(2)}) async-start(), calls=%async_computation.3 | async-start | bytes 3932160 | tf_op jit(solution)/shard_map/reduce_scatter | solution.py:52
  434.6 87.8 %copy-start.5 = (s32[16,24]{1,0:T(8,128)S(1)}, s32[16,24]{1,0:T(8,128)}, u32[]{:S(2)}) copy-start(s32[16,24]{1,0:T(8,128)} %param.9) | copy-start | bytes 4612
  476.0 89.9 %copy-start = (f32[768,1024]{1,0:T(8,128)S(1)}, f32[768,1024]{1,0:T(8,128)}, u32[]{:S(2)}) copy-start(f32[768,1024]{1,0:T(8,128)} %all-gather.7.cloned.1.call-done) | copy-start | bytes 9437188
  478.3 87.6 %all-gather.9.cloned.1.call-start = ((), (), s32[]{:S(2)}) async-start(), calls=%async_computation.4 | async-start | bytes 3932160 | tf_op jit(solution)/shard_map/all_gather | solution.py:53
  522.3 183.5 %reduce-scatter.5.cloned.1.call-start = ((), (), s32[]{:S(2)}) async-start(), calls=%async_computation.5 | async-start | bytes 17825792 | tf_op jit(solution)/shard_map/reduce_scatter | solution.py:101
  604.9 100.9 %copy-start.2 = (f32[1,128,2048]{2,1,0:T(8,128)S(1)}, f32[1,128,2048]{2,1,0:T(8,128)}, u32[]{:S(2)}) copy-start(f32[1,128,2048]{2,1,0:T(8,128)} %param.8) | copy-start | bytes 3145732
Sparse Core Ops, SparseCore 0:
  22.4 35.3 all-gather.10
  59.6 34.4 all-gather.12
  434.7 41.3 all-gather.6
  478.4 43.8 reduce-scatter.2
  524.0 41.8 all-gather.8
  605.1 100.7 reduce-scatter.4
where the time goes:
time: 726 us; the launch traced here: 715 us
  waiting for transfers between devices  284 us (39%)
  other arithmetic  271 us (37%)
  matrix products  60.4 us (8%)
  local copies, waits for them, and re-layouts  51.9 us (7%)
  blocking collectives  27.6 us (4%)
  between operations  20 us (3%)
    another operation x30, other arithmetic, local(): factor = jnp.linalg.cholesky(whole)  172 us
    reduce_scatter x1, waiting for transfers between devices, local(): lax.psum_scatter(spread.reshape(count, column_blocks * BLOCK), 'wide', sc...  99.1 us
    another operation x3, other arithmetic, local(): jax.scipy.linalg.solve_triangular(factor, lower_block[0].T, lower=True)  85.5 us
    all_gather x2, waiting for transfers between devices, gather_in_order(): tiles = lax.all_gather(tiles, axes[k])  56.3 us
    reduce_scatter x1, waiting for transfers between devices, broadcast_by_parts(): own = lax.psum_scatter(padded, axis, scatter_dimension=0, tiled=True)  44 us
    all_gather x1, waiting for transfers between devices, broadcast_by_parts(): lax.all_gather(own, axis, axis=0, tiled=True)[:len(lines)].reshape(x.shape)  43.4 us
    all_gather x1, waiting for transfers between devices, local(): row_part = lax.all_gather(panel, 'gcol', axis=0, tiled=True)  41.4 us
    all_gather x2, blocking collectives, gather_in_order(): tiles = lax.all_gather(tiles, axes[k])  27.6 us
  transfers between devices with their start and end apart: 6, of which 6 were waited for; matrix products, arithmetic and copies ran while one was open for 1% of the time, Pallas kernels for 0%

commit v1 on v0

--- a/solution.py
+++ b/solution.py
@@ -4,6 +4,25 @@
 from jax.sharding import PartitionSpec as P
 
 BLOCK = 128
+
+
+def leaves_lead(mine):
+    dev_axis = "gcol"
+    samples = [mine]
+    chips = lax.axis_size(dev_axis)
+    for c in range(chips - 1):
+        samples.append(
+            lax.ppermute(
+                samples[-1],
+                axis_name=dev_axis,
+                perm=[(idx, (idx + 1) % chips) for idx in range(chips)],
+            )
+        )
+    return jnp.roll(
+        jnp.concatenate(samples[::-1], axis=0),
+        (lax.axis_index(dev_axis) + 1) * mine.shape[0],
+        axis=0,
+    )
 
 
 def cut_rows(length, count):
@@ -62,7 +81,7 @@
         factor, lax.axis_index(("grow", "gcol")) * share, share, 0
     )
     panel = jax.scipy.linalg.solve_triangular(factor, lower_block[0].T, lower=True).T
-    row_part = lax.all_gather(panel, "gcol", axis=0, tiled=True)
+    row_part = leaves_lead(panel)
     column_index = lax.axis_index("gcol")
     col_part = broadcast_by_parts(row_part, "grow", column_index)
     update = lax.dot_general(

time: 726 us -> 740 us (1.019)
  waiting for transfers between devices: 284 us -> 292 us
    ppermute x0 -> x3, waiting for transfers between devices: none -> 52.1 us  [leaves_lead(): lax.ppermute(samples[-1], axis_name=dev_axis, perm=[(idx, (idx + 1) % chi...]
    all_gather x1 -> x0, waiting for transfers between devices: 41.4 us -> none  [local(): row_part = lax.all_gather(panel, 'gcol', axis=0, tiled=True)]
    unnamed x13 -> x22, local copies, waits for them, and re-layouts: 14 us -> 16.2 us
  transfers between devices with their start and end apart: 6 -> 8, of which waited for: 6 -> 8; matrix products, arithmetic and copies ran while one was open for 1% -> 0% of each run, Pallas kernels for 0% -> 0%
where the time goes in v1:
time: 740 us; the launch traced here: 730 us
  waiting for transfers between devices  292 us (39%)
  other arithmetic  271 us (37%)
  matrix products  60.7 us (8%)
  local copies, waits for them, and re-layouts  54.2 us (7%)
  blocking collectives  27.6 us (4%)
  between operations  19.7 us (3%)
    another operation x30, other arithmetic, local(): factor = jnp.linalg.cholesky(whole)  172 us
    reduce_scatter x1, waiting for transfers between devices, local(): lax.psum_scatter(spread.reshape(count, column_blocks * BLOCK), 'wide', sc...  99.1 us
    another operation x3, other arithmetic, local(): jax.scipy.linalg.solve_triangular(factor, lower_block[0].T, lower=True)  85.5 us
    all_gather x2, waiting for transfers between devices, gather_in_order(): tiles = lax.all_gather(tiles, axes[k])  56.3 us
    ppermute x3, waiting for transfers between devices, leaves_lead(): lax.ppermute(samples[-1], axis_name=dev_axis, perm=[(idx, (idx + 1) % chi...  52.1 us
    all_gather x1, waiting for transfers between devices, broadcast_by_parts(): lax.all_gather(own, axis, axis=0, tiled=True)[:len(lines)].reshape(x.shape)  43.3 us
    reduce_scatter x1, waiting for transfers between devices, broadcast_by_parts(): own = lax.psum_scatter(padded, axis, scatter_dimension=0, tiled=True)  40.9 us
    all_gather x2, blocking collectives, gather_in_order(): tiles = lax.all_gather(tiles, axes[k])  27.6 us
  transfers between devices with their start and end apart: 8, of which 8 were waited for; matrix products, arithmetic and copies ran while one was open for 0% of the time, Pallas kernels for 0%

profile of v1, /device:TPU:2, one launch (start us, length us, event | category | flops | bytes accessed | tf_op | source)
XLA Modules:
  0.0 729.6 jit_solution(18411247549285595530)
XLA Ops:
  8.2 14.0 %all_gather.23 = f32[4,32,1024]{2,1,0:T(8,128)} all-gather(f32[1,32,1024]{2,1,0:T(8,128)S(1)} %get-tuple-element.27), channel_id=1, replica_groups=mesh['wide'=16,'grow'=4,'gcol'=4] {'grow'}, dimensions={0}, use_global_device_ids=true | all-gather | bytes 655360 | tf_op jit(solution)/shard_map/all_gather | solution.py:36
  22.3 13.6 %all_gather.26 = f32[4,32,1024]{2,1,0:T(8,128)} all-gather(f32[1,32,1024]{2,1,0:T(8,128)S(1)} %get-tuple-element.28), channel_id=1, replica_groups=mesh['wide'=16,'grow'=4,'gcol'=4] {'gcol'}, dimensions={0}, use_global_device_ids=true | all-gather | bytes 655360 | tf_op jit(solution)/shard_map/all_gather | solution.py:36
  36.0 21.8 %all-gather.8.cloned.1.call-done = f32[16,32,1024]{2,1,0:T(8,128)} async-done(((f32[4,32,1024]{2,1,0:T(8,128)}), f32[16,32,1024]{2,1,0:T(8,128)}) %all-gather.8.cloned.1.call-update) | async-done | bytes 2097168 | tf_op jit(solution)/shard_map/all_gather | solution.py:36
  57.8 1.7 copy.13
  59.5 34.5 %all-gather.10.cloned.1.call-done = f32[16,32,1024]{2,1,0:T(8,128)} async-done(((f32[4,32,1024]{2,1,0:T(8,128)}), f32[16,32,1024]{2,1,0:T(8,128)}) %all-gather.10.cloned.1.call-update) | async-done | bytes 2097168 | tf_op jit(solution)/shard_map/all_gather | solution.py:36
  94.0 4.1 pad_maximum_fusion
  98.1 5.3 copy.14
  103.4 4.4 fusion.2
  107.9 1.9 copy-done
  109.8 11.7 %cholesky.223 = f32[128,128]{1,0:T(8,128)S(1)} custom-call(f32[128,128]{1,0:T(8,128)S(1)} %cholesky.580), custom_call_target="Cholesky" | custom-call | tf_op jit(solution)/shard_map/jit(cholesky)/cholesky | solution.py:78
  121.5 9.8 %custom-call.63 = f32[1,128,128]{1,2,0:T(8,128)S(1)} custom-call(f32[1,128,128]{2,1,0:T(8,128)S(1)} %get-tuple-element.75), custom_call_target="InvertDiagBlocksLowerTriangular" | custom-call | tf_op jit(solution)/shard_map/jit(cholesky)/cholesky | solution.py:78
  131.4 2.5 cholesky.255
  133.9 2.4 constant_dynamic-update-slice_fusion.33
  136.2 1.5 convolution_subtract_fusion
  137.8 12.0 %cholesky.244 = f32[128,128]{1,0:T(8,128)S(1)} custom-call(f32[128,128]{1,0:T(8,128)S(1)} %cholesky.584), custom_call_target="Cholesky" | custom-call | tf_op jit(solution)/shard_map/jit(cholesky)/cholesky | solution.py:78
  150.5 9.8 %custom-call.64 = f32[1,128,128]{1,2,0:T(8,128)S(1)} custom-call(f32[1,128,128]{2,1,0:T(8,128)S(1)} %get-tuple-element.72), custom_call_target="InvertDiagBlocksLowerTriangular" | custom-call | tf_op jit(solution)/shard_map/jit(cholesky)/cholesky | solution.py:78
  161.5 2.1 convolution_subtract_fusion.1
  163.6 11.7 %cholesky.468 = f32[128,128]{1,0:T(8,128)S(1)} custom-call(f32[128,128]{1,0:T(8,128)S(1)} %cholesky.589), custom_call_target="Cholesky" | custom-call | tf_op jit(solution)/shard_map/jit(cholesky)/cholesky | solution.py:78
  176.6 9.8 %custom-call.65 = f32[1,128,128]{1,2,0:T(8,128)S(1)} custom-call(f32[1,128,128]{2,1,0:T(8,128)S(1)} %get-tuple-element.69), custom_call_target="InvertDiagBlocksLowerTriangular" | custom-call | tf_op jit(solution)/shard_map/jit(cholesky)/cholesky | solution.py:78
  187.6 2.3 convolution_subtract_fusion.2
  190.0 11.8 %cholesky.487 = f32[128,128]{1,0:T(8,128)S(1)} custom-call(f32[128,128]{1,0:T(8,128)S(1)} %cholesky.594), custom_call_target="Cholesky" | custom-call | tf_op jit(solution)/shard_map/jit(cholesky)/cholesky | solution.py:78
  203.1 9.8 %custom-call.66 = f32[1,128,128]{1,2,0:T(8,128)S(1)} custom-call(f32[1,128,128]{2,1,0:T(8,128)S(1)} %get-tuple-element.66), custom_call_target="InvertDiagBlocksLowerTriangular" | custom-call | tf_op jit(solution)/shard_map/jit(cholesky)/cholesky | solution.py:78
  214.0 2.3 convolution_subtract_fusion.3
  216.4 11.7 %cholesky.506 = f32[128,128]{1,0:T(8,128)S(1)} custom-call(f32[128,128]{1,0:T(8,128)S(1)} %cholesky.599), custom_call_target="Cholesky" | custom-call | tf_op jit(solution)/shard_map/jit(cholesky)/cholesky | solution.py:78
  229.4 10.0 %custom-call.67 = f32[1,128,128]{1,2,0:T(8,128)S(1)} custom-call(f32[1,128,128]{2,1,0:T(8,128)S(1)} %get-tuple-element.63), custom_call_target="InvertDiagBlocksLowerTriangular" | custom-call | tf_op jit(solution)/shard_map/jit(cholesky)/cholesky | solution.py:78
  240.4 2.3 convolution_subtract_fusion.4
  242.7 11.7 %cholesky.526 = f32[128,128]{1,0:T(8,128)S(1)} custom-call(f32[128,128]{1,0:T(8,128)S(1)} %cholesky.604), custom_call_target="Cholesky" | custom-call | tf_op jit(solution)/shard_map/jit(cholesky)/cholesky | solution.py:78
  255.7 9.8 %custom-call.68 = f32[1,128,128]{1,2,0:T(8,128)S(1)} custom-call(f32[1,128,128]{2,1,0:T(8,128)S(1)} %get-tuple-element.60), custom_call_target="InvertDiagBlocksLowerTriangular" | custom-call | tf_op jit(solution)/shard_map/jit(cholesky)/cholesky | solution.py:78
  266.4 2.0 convolution_subtract_fusion.5
  268.5 12.1 %cholesky.546 = f32[128,128]{1,0:T(8,128)S(1)} custom-call(f32[128,128]{1,0:T(8,128)S(1)} %cholesky.609), custom_call_target="Cholesky" | custom-call | tf_op jit(solution)/shard_map/jit(cholesky)/cholesky | solution.py:78
  281.8 9.8 %custom-call.69 = f32[1,128,128]{1,2,0:T(8,128)S(1)} custom-call(f32[1,128,128]{2,1,0:T(8,128)S(1)} %get-tuple-element.57), custom_call_target="InvertDiagBlocksLowerTriangular" | custom-call | tf_op jit(solution)/shard_map/jit(cholesky)/cholesky | solution.py:78
  292.5 1.8 convolution_subtract_fusion.13
  294.3 11.7 %cholesky.564 = f32[128,128]{1,0:T(8,128)S(1)} custom-call(f32[128,128]{1,0:T(8,128)S(1)} %convolution_subtract_fusion.13), custom_call_target="Cholesky" | custom-call | tf_op jit(solution)/shard_map/jit(cholesky)/cholesky | solution.py:78
  313.0 6.7 fusion.3
  319.7 23.2 %while.1 = (s32[]{:T(128)}, f32[1024,1024]{1,0:T(8,128)}, s32[8,2]{0,1:T(2,128)S(1)}, f32[8,128,128]{2,1,0:T(8,128)S(1)}, s32[]{:T(128)}) while((s32[]{:T(128)}, f32[1024,1024]{1,0:T(8,128)}, s32[8,2]{0,1:T(2,128)S(1)}, f32[8,128,128]{2,1,0:T(8,128)S(1)}, s32[]{:T(128)}) %tuple.67), condition=%wide.while_cond, body=%wide.while_body.sunk | while | flops 2 | bytes 131189 | solution.py:83
  320.3 2.3 bitcast_dynamic-update-slice_fusion.2
  323.2 2.3 bitcast_dynamic-update-slice_fusion.2
  326.1 2.3 bitcast_dynamic-update-slice_fusion.2
  329.0 2.3 bitcast_dynamic-update-slice_fusion.2
  331.9 2.3 bitcast_dynamic-update-slice_fusion.2
  334.8 2.3 bitcast_dynamic-update-slice_fusion.2
  337.7 2.3 bitcast_dynamic-update-slice_fusion.2
  340.6 2.2 bitcast_dynamic-update-slice_fusion.2
  342.9 78.8 %custom-call.70 = f32[8,128,128]{1,2,0:T(8,128)S(1)} custom-call(f32[8,128,128]{2,1,0:T(8,128)S(1)} %get-tuple-element.10), custom_call_target="InvertDiagBlocksLowerTriangular" | custom-call | tf_op jit(solution)/shard_map/jit(_solve_triangular)/triangular_solve | solution.py:83
  428.1 1.6 convolution_subtract_fusion.8
  429.9 1.6 convolution_subtract_fusion.7
  431.7 1.8 convolution_subtract_fusion.6
  433.8 1.5 collective-permute-start
  435.3 17.8 %collective-permute-done = f32[192,1024]{1,0:T(8,128)S(1)} collective-permute-done((f32[192,1024]{1,0:T(8,128)S(1)}, f32[192,1024]{1,0:T(8,128)S(1)}, u32[]{:S(2)}, u32[]{:S(2)}) %collective-permute-start) | collective-permute-done | bytes 786464 | tf_op jit(solution)/shard_map/ppermute | solution.py:15
  453.1 1.5 collective-permute-start.1
  454.6 17.0 %collective-permute-done.1 = f32[192,1024]{1,0:T(8,128)S(1)} collective-permute-done((f32[192,1024]{1,0:T(8,128)S(1)}, f32[192,1024]{1,0:T(8,128)S(1)}, u32[]{:S(2)}, u32[]{:S(2)}) %collective-permute-start.1) | collective-permute-done | bytes 786464 | tf_op jit(solution)/shard_map/ppermute | solution.py:15
  473.0 17.3 %collective-permute-done.2 = f32[192,1024]{1,0:T(8,128)S(1)} collective-permute-done((f32[192,1024]{1,0:T(8,128)S(1)}, f32[192,1024]{1,0:T(8,128)S(1)}, u32[]{:S(2)}, u32[]{:S(2)}) %collective-permute-start.2) | collective-permute-done | bytes 786464 | tf_op jit(solution)/shard_map/ppermute | solution.py:15
  490.8 2.7 copy-done.1
  493.5 2.1 dynamic-slice_select_fusion
  495.7 40.9 %reduce-scatter.3.cloned.1.call-done = f32[192,1024]{1,0:T(8,128)} async-done(((f32[768,1024]{1,0:T(8,128)}), f32[192,1024]{1,0:T(8,128)}) %reduce-scatter.3.cloned.1.call-update) | async-done | bytes 786448 | tf_op jit(solution)/shard_map/reduce_scatter | solution.py:71
  536.7 43.3 %all-gather.6.cloned.1.call-done = f32[768,1024]{1,0:T(8,128)} async-done(((f32[192,1024]{1,0:T(8,128)}), f32[768,1024]{1,0:T(8,128)}) %all-gather.6.cloned.1.call-update) | async-done | bytes 3145744 | tf_op jit(solution)/shard_map/all_gather | solution.py:72
  580.1 11.7 %bitcast_subtract_fusion = f32[768,768]{1,0:T(8,128)} fusion(f32[1,768,768]{2,1,0:T(8,128)S(1)} %copy-done.3, f32[768,1024]{1,0:T(8,128)} %all-gather.6.cloned.1.call-done, f32[1536,1024]{1,0:T(8,128)} %copy-done.1, s32[]{:T(128)S(6)} %select_n.56), kind=kOutput, calls=%fused_computation.16 | convolution fusion | flops 7248347136 | bytes 11010052 | tf_op jit(solution)/shard_map/dot_general | solution.py:87
  591.8 2.5 reshape.103
  594.3 4.0 fusion.4
  598.4 9.9 %fusion = f32[16,16,128,128]{3,0,2,1:T(8,128)S(1)} fusion(f32[16,128,6,128]{3,0,2,1:T(8,128)S(1)} %fusion.4, s32[6]{0:T(128)S(1)} %fusion.76), kind=kOutput, calls=%fused_computation.3 | convolution fusion | flops 301989984 | bytes 23068696 | tf_op jit(solution)/shard_map/pxcy,qc->pxqy/dot_general | solution.py:119
  608.3 11.2 %copy.25 = f32[256,8,16,128]{3,1,2,0:T(8,128)} copy(f32[256,8,16,128]{3,2,1,0:T(8,128)S(1)} %bitcast.142) | data formatting | bytes 33554432
  619.5 1.8 dynamic-slice_bitcast_fusion
  621.3 99.1 %reduce-scatter.5.cloned.1.call-done = f32[128,2048]{1,0:T(8,128)} async-done(((f32[2048,2048]{1,0:T(8,128)}), f32[128,2048]{1,0:T(8,128)}) %reduce-scatter.5.cloned.1.call-update) | async-done | bytes 1048592 | tf_op jit(solution)/shard_map/reduce_scatter | solution.py:120
  720.4 2.3 bitcast_add_fusion.1
  (94 shorter events, 30.5 us)
Async XLA Ops:
  7.2 50.6 %all-gather.8.cloned.1.call-start = ((), (), s32[]{:S(2)}) async-start(), calls=%async_computation.5 | async-start | bytes 2621440 | tf_op jit(solution)/shard_map/all_gather | solution.py:36
  22.3 71.7 %all-gather.10.cloned.1.call-start = ((), (), s32[]{:S(2)}) async-start(), calls=%async_computation.6 | async-start | bytes 2621440 | tf_op jit(solution)/shard_map/all_gather | solution.py:36
  35.9 500.6 %reduce-scatter.3.cloned.1.call-start = ((), (), s32[]{:S(2)}) async-start(), calls=%async_computation.2 | async-start | bytes 3932160 | tf_op jit(solution)/shard_map/reduce_scatter | solution.py:71
  107.9 1.9 copy-start
  313.0 108.7 %copy-start.5 = (f32[1,192,1024]{2,1,0:T(8,128)S(1)}, f32[1,192,1024]{2,1,0:T(8,128)}, u32[]{:S(2)}) copy-start(f32[1,192,1024]{2,1,0:T(8,128)} %param.6) | copy-start | bytes 2359300
  433.8 57.0 %copy-start.2 = (f32[1024,192]{0,1:T(8,128)}, f32[1024,192]{0,1:T(8,128)S(1)}, u32[]{:S(2)}) copy-start(f32[1024,192]{0,1:T(8,128)S(1)} %convolution_dynamic-update-slice_fusion.5) | copy-start | bytes 2359300
  433.8 19.4 %collective-permute-start = (f32[192,1024]{1,0:T(8,128)S(1)}, f32[192,1024]{1,0:T(8,128)S(1)}, u32[]{:S(2)}, u32[]{:S(2)}) collective-permute-start(f32[192,1024]{1,0:T(8,128)S(1)} %bitcast.146), channel_id=1, source_target_pairs={{0,1},{1,2},{2,3},{3,0},{4,5},{5,6},{6,7},{7,4},{8,9},{9,10},{10,1... | collective-permute-start | bytes 2359304 | tf_op jit(solution)/shard_map/ppermute | solution.py:15
  453.1 18.5 %collective-permute-start.1 = (f32[192,1024]{1,0:T(8,128)S(1)}, f32[192,1024]{1,0:T(8,128)S(1)}, u32[]{:S(2)}, u32[]{:S(2)}) collective-permute-start(f32[192,1024]{1,0:T(8,128)S(1)} %collective-permute-done), channel_id=1, source_target_pairs={{0,1},{1,2},{2,3},{3,0},{4,5},{5,6},{6,7},{7,4},{8,9},{9,10},{10,1... | collective-permute-start | bytes 2359304 | tf_op jit(solution)/shard_map/ppermute | solution.py:15
  471.6 18.7 %collective-permute-start.2 = (f32[192,1024]{1,0:T(8,128)S(1)}, f32[192,1024]{1,0:T(8,128)S(1)}, u32[]{:S(2)}, u32[]{:S(2)}) collective-permute-start(f32[192,1024]{1,0:T(8,128)S(1)} %collective-permute-done.1), channel_id=1, source_target_pairs={{0,1},{1,2},{2,3},{3,0},{4,5},{5,6},{6,7},{7,4},{8,9},{9,10},{10,1... | collective-permute-start | bytes 2359304 | tf_op jit(solution)/shard_map/ppermute | solution.py:15
  490.8 2.7 copy-start.1
  493.5 43.1 %copy-start.6 = (s32[16,24]{1,0:T(8,128)S(1)}, s32[16,24]{1,0:T(8,128)}, u32[]{:S(2)}) copy-start(s32[16,24]{1,0:T(8,128)} %param.9) | copy-start | bytes 4612
  493.5 86.6 %copy-start.3 = (f32[1,768,768]{2,1,0:T(8,128)S(1)}, f32[1,768,768]{2,1,0:T(8,128)}, u32[]{:S(2)}) copy-start(f32[1,768,768]{2,1,0:T(8,128)} %param.7) | copy-start | bytes 7077892
  495.6 84.5 %all-gather.6.cloned.1.call-start = ((), (), s32[]{:S(2)}) async-start(), calls=%async_computation.3 | async-start | bytes 3932160 | tf_op jit(solution)/shard_map/all_gather | solution.py:72
  536.6 183.8 %reduce-scatter.5.cloned.1.call-start = ((), (), s32[]{:S(2)}) async-start(), calls=%async_computation.4 | async-start | bytes 17825792 | tf_op jit(solution)/shard_map/reduce_scatter | solution.py:120
  619.5 100.9 %copy-start.4 = (f32[1,128,2048]{2,1,0:T(8,128)S(1)}, f32[1,128,2048]{2,1,0:T(8,128)}, u32[]{:S(2)}) copy-start(f32[1,128,2048]{2,1,0:T(8,128)} %param.8) | copy-start | bytes 3145732
Sparse Core Ops, SparseCore 0:
  22.4 35.3 all-gather.7
  59.6 34.4 all-gather.9
  495.7 40.7 reduce-scatter.2
  538.2 41.8 all-gather.5
  619.6 100.6 reduce-scatter.4
